TPU v7x, 128 devices: a whole 4x4x4 slice. The times are simulated.
128 devices in a mesh: spec: 8 (over x_hi, y), neuron: 16 (over x_lo, z, core).
Axes of the slice: x: 4 (x_hi: 2, x_lo: 2; x = x_hi * 2 + x_lo), y: 4, z: 4, core: 2. Of those that a mesh axis runs over, the one named last changes fastest.
Arguments:
- panel: float32 [1536, 16384], P('spec', 'neuron'), may hold values from -6 to 6
- weight: float32 [16384, 16384], P('neuron', 'spec'), may hold values from -0.046875 to 0.046875
- layer_bias: float32 [16384], P('neuron'), may hold values from -0.06 to 0.06
- act_center: float32 [2, 16384], P(None, 'neuron'), may hold values from -6 to 6
- act_radius: float32 [2, 16384], P(None, 'neuron'), may hold values from 0.05 to 1
- alpha: float32 [2, 16384], P(None, 'neuron'), may hold values from 0 to 1
- in_center: float32 [2, 16384], P(None, 'spec'), may hold values from -0.12 to 0.12
- in_radius: float32 [2, 16384], P(None, 'spec'), may hold values from 1e-07 to 0.005
- bias_in: float32 [1536], replicated, may hold values from -6 to 6
- spec_neuron: int32 [2, 384], replicated, may hold values from 0 to 16383, as said below
- prior_lower: float32 [2, 16384], P(None, 'neuron'), may hold values from -7 to 0.5
- prior_upper: float32 [2, 16384], P(None, 'neuron'), may hold values from -0.5 to 7
Outputs:
- coef_next: float32 [1536, 16384], P('neuron', 'spec')
- lower_bound: float32 [1536], P('neuron')
- new_slope: float32 [2, 16384], P(None, 'neuron')
- new_shift: float32 [2, 16384], P(None, 'neuron')
Inputs may be any that keep to these rules, and one draw needn't show every extreme that they name: `spec_neuron`: each sample's row names 384 different neurons.
All inputs are finite; a program needn't handle non-finite values.
Results may differ from a plain program's by a relative error of at most 0.0003.
Values sent between devices are 32-bit elements; how exact they have to be, the bound alone decides.
A program may use at most 128 MiB of HBM per device.

v0:
```python
import jax
import jax.numpy as jnp
from jax import lax
from jax.sharding import PartitionSpec as P


def pick_rows(sample_table, row_sample):
    return jnp.where(row_sample[:, None] == 0, sample_table[0][None, :], sample_table[1][None, :])


def concretize(coefs, center, radius, row_sample):
    return jnp.sum(
        coefs * pick_rows(center, row_sample) - jnp.abs(coefs) * pick_rows(radius, row_sample),
        axis=1,
    )


def refresh_slope(new_low, new_high):
    rising = jax.nn.relu(new_high)
    falling = jax.nn.relu(-new_low)
    denom = rising + falling
    unstable = jnp.logical_and(new_low < 0.0, new_high > 0.0)
    safe = jnp.where(unstable, denom, 1.0)
    ratio = rising / safe
    slope = jnp.where(new_low >= 0.0, 1.0, jnp.where(new_high <= 0.0, 0.0, ratio))
    return (slope, slope * falling)


def per_device(
    panel,
    weight,
    layer_bias,
    act_center,
    act_radius,
    alpha,
    in_center,
    in_radius,
    bias_in,
    spec_neuron,
    prior_lower,
    prior_upper,
):
    own_rows, own_cols = panel.shape
    spec_count = spec_neuron.shape[1]
    sample_rows = 2 * spec_count
    total_rows = 4 * spec_count
    first_row = lax.axis_index("spec") * own_rows
    row_sample = (first_row + jnp.arange(own_rows, dtype=jnp.int32)) // sample_rows
    act_low = act_center - act_radius
    act_high = act_center + act_radius
    upper_part = jax.nn.relu(act_high)
    lower_part = jax.nn.relu(-act_low)
    up_slope = upper_part / (upper_part + lower_part)
    up_shift = up_slope * lower_part
    low_slope = jnp.where(act_low >= 0.0, 1.0, jnp.where(act_high <= 0.0, 0.0, alpha))
    relaxed = pick_rows(low_slope, row_sample) * jnp.maximum(panel, 0.0) + pick_rows(
        up_slope, row_sample
    ) * jnp.minimum(panel, 0.0)
    shift_local = jnp.dot(
        relaxed, layer_bias, precision=lax.Precision.HIGHEST, preferred_element_type=jnp.float32
    )
    shift_local = shift_local + jnp.sum(
        jnp.minimum(panel, 0.0) * pick_rows(up_shift, row_sample), axis=1
    )
    shift_rows = lax.psum(shift_local, "neuron")
    gathered, shift_all = (
        lax.all_gather(relaxed, "spec", axis=0, tiled=True),
        lax.all_gather(shift_rows, "spec", axis=0, tiled=True),
    )
    share_rows = total_rows // lax.axis_size("neuron")
    start_row = lax.axis_index("neuron") * share_rows
    product = jnp.dot(
        gathered, weight, precision=lax.Precision.HIGHEST, preferred_element_type=jnp.float32
    )
    product = lax.psum(product, "neuron")
    all_sample = jnp.arange(total_rows, dtype=jnp.int32) // sample_rows
    partial_sum = concretize(product, in_center, in_radius, all_sample)
    bounds_all = lax.psum(partial_sum, "spec") + shift_all + bias_in
    coef_next = lax.dynamic_slice_in_dim(product, start_row, share_rows, 0)
    lower_bound = lax.dynamic_slice_in_dim(bounds_all, start_row, share_rows, 0)
    grouped = bounds_all.reshape(2, 2, spec_count)
    low_found = grouped[:, 0, :]
    high_found = -grouped[:, 1, :]
    column_ids = lax.axis_index("neuron") * own_cols + jnp.arange(own_cols, dtype=jnp.int32)
    matched = spec_neuron[:, :, None] == column_ids[None, None, :]
    low_comp = jnp.sum(jnp.where(matched, low_found[:, :, None], 0.0), axis=1)
    high_comp = jnp.sum(jnp.where(matched, high_found[:, :, None], 0.0), axis=1)
    touched = jnp.any(matched, axis=1)
    new_low = jnp.where(touched, jnp.maximum(prior_lower, low_comp), prior_lower)
    new_high = jnp.where(touched, jnp.minimum(prior_upper, high_comp), prior_upper)
    new_slope, new_shift = refresh_slope(new_low, new_high)
    return (coef_next, lower_bound, new_slope, new_shift)


def solution(mesh):
    in_specs = (
        P("spec", "neuron"),
        P("neuron", "spec"),
        P("neuron"),
        P(None, "neuron"),
        P(None, "neuron"),
        P(None, "neuron"),
        P(None, "spec"),
        P(None, "spec"),
        P(),
        P(),
        P(None, "neuron"),
        P(None, "neuron"),
    )
    out_specs = (P("neuron", "spec"), P("neuron"), P(None, "neuron"), P(None, "neuron"))
    return jax.shard_map(
        per_device, mesh=mesh, in_specs=in_specs, out_specs=out_specs, check_vma=False
    )
```

profile of v0, /device:TPU:1, one launch (start us, length us, event | category | flops | bytes accessed | tf_op | source)
XLA Modules:
  0.0 343.3 jit_solution(13760896037696523459)
XLA Ops:
  7.2 0.0 copy-start
  7.2 0.0 all-gather.2.cloned.1.call-start
  7.2 0.8 fusion.8
  8.1 2.4 multiply_reduce_fusion
  10.4 0.0 all-gather.2.cloned.1.call-update
  10.5 0.0 all-reduce.3.cloned.1.call-start
  10.5 92.0 %all-gather.2.cloned.1.call-done = f32[1536,1024]{1,0:T(8,128)} async-done(((f32[192,1024]{1,0:T(8,128)}), f32[1536,1024]{1,0:T(8,128)}) %all-gather.2.cloned.1.call-update) | async-done | bytes 6291472 | tf_op jit(solution)/shard_map/all_gather | solution.py:67
  102.5 45.5 %fusion.15 = f32[1536,2048]{1,0:T(8,128)} fusion(f32[1536,1024]{1,0:T(8,128)} %all-gather.2.cloned.1.call-done, f32[1024,2048]{1,0:T(8,128)} %param.13), kind=kOutput, calls=%fused_computation.42 | convolution fusion | flops 38654705664 | bytes 27262976 | tf_op jit(solution)/shard_map/dot_general | solution.py:72
  148.0 0.0 copy-start.1
  148.0 0.0 copy-start.8
  148.0 0.0 copy-start.4
  148.0 0.0 copy-start.2
  148.0 0.0 copy-start.3
  148.1 0.0 all-reduce.3.cloned.1.call-update
  148.1 0.0 copy-start.5
  148.1 0.0 copy-start.6
  148.1 0.0 copy-start.7
  148.1 0.0 copy-done
  148.1 1.0 copy-done.1
  149.2 0.7 fusion.16
  149.9 0.0 copy-done.8
  149.9 0.6 dynamic-slice
  151.1 28.0 %psum.23 = f32[192]{0:T(256)S(1)} all-reduce(f32[192]{0:T(256)S(1)} %add.67), channel_id=1, replica_groups=mesh['spec'=8,'neuron'=16] {'neuron'}, use_global_device_ids=true, to_apply=%region_4.5 | all-reduce | flops 192 | bytes 1536 | tf_op jit(solution)/shard_map/psum | solution.py:65
  179.1 0.0 copy-done.4
  179.1 0.5 compare_reduce_fusion
  179.6 0.0 copy-done.2
  179.7 0.0 copy-done.3
  179.7 124.9 %all-reduce.3.cloned.1.call-done = f32[1536,2048]{1,0:T(8,128)} async-done(((f32[1536,2048]{1,0:T(8,128)}), f32[1536,2048]{1,0:T(8,128)}) %all-reduce.3.cloned.1.call-update) | async-done | bytes 12582928 | tf_op jit(solution)/shard_map/psum | solution.py:75
  304.6 7.0 %subtract_reduce_fusion = f32[1536]{0:T(1024)S(1)} fusion(f32[1536,2048]{1,0:T(8,128)} %all-reduce.3.cloned.1.call-done, f32[2048]{0:T(1024)S(1)} %bitcast.27, f32[2048]{0:T(1024)S(1)} %bitcast.26, f32[2048]{0:T(1024)S(1)} %bitcast.25, f32[2048]{0:T(1024)S(1)} %bitcast.24, pred[1536]{0:T(1024)(128)(4,1)S(1)} %fusion.2), kind=kLoop, calls=%fused_computation | loop fusion | flops 22018560 | bytes 12623360 | tf_op jit(solution)/shard_map/reduce_sum | solution.py:12
  311.7 0.2 add_dynamic-update-slice_fusion
  311.9 20.6 %psum.24 = f32[1536]{0:T(1024)S(1)} all-reduce(f32[1536]{0:T(1024)S(1)} %add_dynamic-update-slice_fusion), channel_id=1, replica_groups=mesh['spec'=8,'neuron'=16] {'spec'}, use_global_device_ids=true, to_apply=%region_2.3 | all-reduce | flops 1536 | bytes 12288 | tf_op jit(solution)/shard_map/psum | solution.py:78
  332.5 0.0 copy-done.5
  332.5 0.6 dynamic_slice.7
  333.1 0.6 fusion
  333.7 0.0 copy-done.6
  333.8 0.0 copy-done.7
  333.8 0.6 fusion.6
  334.4 2.1 constant_dynamic-slice_fusion
  (13 shorter events, 0.1 us)
Async XLA Ops:
  7.2 141.0 %copy-start = (f32[1024]{0:T(1024)S(1)}, f32[1024]{0:T(1024)}, u32[]{:S(2)}) copy-start(f32[1024]{0:T(1024)} %param.14) | copy-start | bytes 12292
  7.2 95.3 %all-gather.2.cloned.1.call-start = ((), (), s32[]{:S(2)}) async-start(), calls=%async_computation | async-start | bytes 7077888 | tf_op jit(solution)/shard_map/all_gather | solution.py:67
  10.5 294.2 %all-reduce.3.cloned.1.call-start = ((), (), s32[]{:S(2)}) async-start(), calls=%async_computation.1 | async-start | bytes 25165824 | tf_op jit(solution)/shard_map/psum | solution.py:75
  148.0 1.1 copy-start.1
  148.0 1.9 copy-start.8
  148.0 31.1 %copy-start.4 = (s32[2,384]{1,0:T(2,128)S(1)}, s32[2,384]{1,0:T(2,128)}, u32[]{:S(2)}) copy-start(s32[2,384]{1,0:T(2,128)} %param.21) | copy-start | bytes 9220
  148.0 31.6 %copy-start.2 = (f32[2,2048]{1,0:T(2,128)S(1)}, f32[2,2048]{1,0:T(2,128)}, u32[]{:S(2)}) copy-start(f32[2,2048]{1,0:T(2,128)} %param.18) | copy-start | bytes 49156
  148.0 31.6 %copy-start.3 = (f32[2,2048]{1,0:T(2,128)S(1)}, f32[2,2048]{1,0:T(2,128)}, u32[]{:S(2)}) copy-start(f32[2,2048]{1,0:T(2,128)} %param.19) | copy-start | bytes 49156
  148.1 184.4 %copy-start.5 = (f32[1536]{0:T(1024)S(1)}, f32[1536]{0:T(1024)}, u32[]{:S(2)}) copy-start(f32[1536]{0:T(1024)} %param.20) | copy-start | bytes 18436
  148.1 185.7 %copy-start.6 = (f32[2,1024]{1,0:T(2,128)S(1)}, f32[2,1024]{1,0:T(2,128)}, u32[]{:S(2)}) copy-start(f32[2,1024]{1,0:T(2,128)} %param.22) | copy-start | bytes 24580
  148.1 185.6 %copy-start.7 = (f32[2,1024]{1,0:T(2,128)S(1)}, f32[2,1024]{1,0:T(2,128)}, u32[]{:S(2)}) copy-start(f32[2,1024]{1,0:T(2,128)} %param.23) | copy-start | bytes 24580
Sparse Core Ops, SparseCore 0:
  10.9 91.5 all-gather.1
  148.2 156.3 all-reduce.2
where the time goes:
time: 348 us; the launch traced here: 343 us
  waiting for transfers between devices  217 us (62%)
  blocking collectives  48.5 us (14%)
  matrix products  46.2 us (13%)
  between operations  14.9 us (4%)
  other arithmetic  12.2 us (4%)
  local copies, waits for them, and re-layouts  4.39 us (1%)
    psum x1, waiting for transfers between devices, per_device(): product = lax.psum(product, 'neuron')  125 us
    all_gather x1, waiting for transfers between devices, per_device(): lax.all_gather(relaxed, 'spec', axis=0, tiled=True)  92 us
    dot_general x1, matrix products, per_device(): jnp.dot(gathered, weight, precision=lax.Precision.HIGHEST, preferred_elem...  45.5 us
    psum x1, blocking collectives, per_device(): shift_rows = lax.psum(shift_local, 'neuron')  28 us
    psum x1, blocking collectives, per_device(): bounds_all = lax.psum(partial_sum, 'spec') + shift_all + bias_in  20.6 us
    reduce_sum x1, other arithmetic, concretize(): jnp.sum(coefs * pick_rows(center, row_sample) - jnp.abs(coefs) * pick_row...  7.04 us
  transfers between devices with their start and end apart: 2, of which 2 were waited for; matrix products, arithmetic and copies ran while one was open for 1% of the time, Pallas kernels for 0%

commit v1 on v0

v1 whole, which is shorter than its diff:
```python
import functools

import jax
import jax.numpy as jnp
from jax import lax
from jax.experimental import pallas as pl
from jax.experimental.pallas import tpu as pltpu
from jax.sharding import PartitionSpec as P

MESH = pl.DeviceIdType.MESH
F32 = jnp.float32
BF16 = jnp.bfloat16
XH, Y, XL, Z = 2, 4, 2, 4
NSPEC, NNEUR = XH * Y, XL * Z * 2
LANES = 128

(S_XH, S_OWN_P, S_OWN_M, S_PAR_P, S_PAR_M, S_F0_P, S_F1_P, S_F0_M, S_F1_M,
 S_CORE, S_Z1_P, S_Z1_M, S_Z2_P, S_Z2_M, S_XL) = range(15)
NCOPY = 15

LOOK_XH = 4
LOOK_OWN = 3
LOOK_PAR = 2
TILE_N = 512
W_ROWS = 256


def fold_lanes(v):
    out = v[:, 0:LANES]
    for g in range(1, v.shape[1] // LANES):
        out = out + v[:, g * LANES:(g + 1) * LANES]
    return out


def rows_to_lanes(t):
    return lax.dot_general(
        jnp.ones((8, LANES), F32), t, (((1,), (1,)), ((), ())),
        precision=lax.Precision.HIGHEST, preferred_element_type=F32)


def kernel(panel, weight, lbias, ac, ar, al, ic, ir, bias, names, plow, phigh,
           coef, lbound, nslope, nshift,
           pan, wst, whi, wlo, g, asp, prod, cr, z1p, z1m, z2p, z2m, xb,
           ts, tb, shs, sb, ssum, pb, bb, onehot, touched,
           dsem, ssem, rsem, shs_s, shs_r, pb_s, pb_r, bb_s, bb_r):
    chunks = g.shape[0]
    kdim, ndim = whi.shape
    half = ndim // 2
    s = lax.axis_index("spec")
    n = lax.axis_index("neuron")
    xh, y = s // Y, s % Y
    xl, z, k = n // (2 * Z), (n // 2) % Z, n % 2
    yp, ym, y2 = (y + 1) % Y, (y + 3) % Y, (y + 2) % Y
    zp, zm, z2 = (z + 1) % Z, (z + 3) % Z, (z + 2) % Z

    dev_xh = ((1 - xh) * Y + y, n)
    dev_yp, dev_ym = (xh * Y + yp, n), (xh * Y + ym, n)
    dev_core = (s, xl * 2 * Z + z * 2 + (1 - k))
    dev_zp, dev_zm = (s, xl * 2 * Z + zp * 2 + k), (s, xl * 2 * Z + zm * 2 + k)
    dev_xl = (s, (1 - xl) * 2 * Z + z * 2 + k)

    load_panel = pltpu.make_async_copy(panel, pan, dsem.at[0])
    load_panel.start()
    pieces = kdim // W_ROWS
    w_loads = [
        pltpu.make_async_copy(weight.at[pl.ds(i * W_ROWS, W_ROWS)], wst.at[i], dsem.at[1 + i])
        for i in range(pieces)]
    for w_load in w_loads:
        w_load.start()

    barrier = pltpu.get_barrier_semaphore()
    for j in range(1, NSPEC):
        pl.semaphore_signal(barrier, inc=1, device_id=((s + j) % NSPEC, n), device_id_type=MESH)
    for j in range(1, NNEUR):
        pl.semaphore_signal(barrier, inc=1, device_id=(s, (n + j) % NNEUR), device_id_type=MESH)

    def pick(ref, i):
        return jnp.where(i == 0, ref[0:1, :], ref[1:2, :])

    center, radius = pick(ac, xh), pick(ar, xh)
    act_low, act_high = center - radius, center + radius
    upper, lower = jnp.maximum(act_high, 0.0), jnp.maximum(-act_low, 0.0)
    up_slope = upper / (upper + lower)
    up_shift = up_slope * lower
    low_slope = jnp.where(act_low >= 0.0, 1.0, jnp.where(act_high <= 0.0, 0.0, pick(al, xh)))
    lb = lbias[...]
    ts[...] = jnp.zeros_like(ts)
    tb[...] = jnp.zeros_like(tb)
    load_panel.wait()

    def relax(c, carry):
        for h in range(2):
            p = pan[h, pl.ds(pl.multiple_of(c * 8, 8), 8), :]
            neg = jnp.minimum(p, 0.0)
            rel = low_slope * jnp.maximum(p, 0.0) + up_slope * neg
            g[c, xh, y, h] = rel
            ts[h, pl.ds(pl.multiple_of(c * 8, 8), 8), :] = fold_lanes(rel * lb + neg * up_shift)
        return carry

    lax.fori_loop(0, chunks, relax, 0)
    pl.semaphore_wait(barrier, NSPEC + NNEUR - 2)

    def rc(src, dst, kind, c, dev):
        return pltpu.make_async_remote_copy(
            src_ref=src, dst_ref=dst, send_sem=ssem.at[c, kind], recv_sem=rsem.at[c, kind],
            device_id=dev, device_id_type=MESH)

    def block_copy(kind, c, bx, by, dev):
        return rc(g.at[c, bx, by], g.at[c, bx, by], kind, c, dev)

    def half_copy(kind, c, bx, by, h, dev):
        return rc(g.at[c, bx, by, h], g.at[c, bx, by, h], kind, c, dev)

    def xh_send(c): return block_copy(S_XH, c, xh, y, dev_xh)
    def xh_recv(c): return block_copy(S_XH, c, 1 - xh, y, dev_xh)

    def own_send(c):
        return [block_copy(S_OWN_P, c, xh, y, dev_yp), block_copy(S_OWN_M, c, xh, y, dev_ym)]

    def own_recv(c):
        return [block_copy(S_OWN_P, c, xh, ym, dev_yp), block_copy(S_OWN_M, c, xh, yp, dev_ym)]

    def par_send(c):
        return [block_copy(S_PAR_P, c, 1 - xh, y, dev_yp), block_copy(S_PAR_M, c, 1 - xh, y, dev_ym)]

    def par_recv(c):
        return [block_copy(S_PAR_P, c, 1 - xh, ym, dev_yp), block_copy(S_PAR_M, c, 1 - xh, yp, dev_ym)]

    def fwd_send(c):
        return [half_copy(S_F0_P, c, xh, ym, 0, dev_yp), half_copy(S_F0_M, c, xh, yp, 1, dev_ym),
                half_copy(S_F1_P, c, 1 - xh, ym, 0, dev_yp), half_copy(S_F1_M, c, 1 - xh, yp, 1, dev_ym)]

    def fwd_recv(c):
        return [half_copy(S_F0_P, c, xh, y2, 0, dev_yp), half_copy(S_F0_M, c, xh, y2, 1, dev_ym),
                half_copy(S_F1_P, c, 1 - xh, y2, 0, dev_yp), half_copy(S_F1_M, c, 1 - xh, y2, 1, dev_ym)]

    def core_copy(c):
        return rc(prod.at[c, :, :, 1 - k], cr.at[c], S_CORE, c, dev_core)

    def z1_copy(c):
        return [rc(prod.at[c, :, z2, k, :, pl.ds(0, half)], z1p.at[c], S_Z1_P, c, dev_zp),
                rc(prod.at[c, :, z2, k, :, pl.ds(half, half)], z1m.at[c], S_Z1_M, c, dev_zm)]

    def z2_copy(c):
        return [rc(prod.at[c, :, zp, k], z2p.at[c], S_Z2_P, c, dev_zp),
                rc(prod.at[c, :, zm, k], z2m.at[c], S_Z2_M, c, dev_zm)]

    def xl_copy(c):
        return rc(prod.at[c, 1 - xl, z, k], xb.at[c], S_XL, c, dev_xl)

    def start(copies):
        for copy in copies:
            copy.start()

    def wait_recv(copies):
        for copy in copies:
            copy.wait_recv()

    for c in range(min(LOOK_OWN, chunks)):
        xh_send(c).start()
        start(own_send(c))
    for c in range(LOOK_OWN, min(LOOK_XH, chunks)):
        xh_send(c).start()

    for h in range(2):
        shs[h] = rows_to_lanes(ts[h])

    def shs_copy(h):
        return pltpu.make_async_remote_copy(
            src_ref=shs.at[h], dst_ref=sb.at[n], send_sem=shs_s.at[h], recv_sem=shs_r.at[n],
            device_id=(s, 2 * s + h), device_id_type=MESH)

    for h in range(2):
        @pl.when(n != 2 * s + h)
        def _(h=h):
            shs_copy(h).start()

        @pl.when(n == 2 * s + h)
        def _(h=h):
            sb[n] = shs[h]

    def split_piece(i):
        def body(r, carry):
            w = wst[i, pl.ds(pl.multiple_of(r * 16, 16), 16), :]
            hi = w.astype(BF16)
            rows = pl.ds(pl.multiple_of(i * W_ROWS + r * 16, 16), 16)
            whi[rows, :] = hi
            wlo[rows, :] = (w - hi.astype(F32)).astype(BF16)
            return carry
        w_loads[i].wait()
        lax.fori_loop(0, W_ROWS // 16, body, 0)

    split_piece(0)
    for c in range(min(LOOK_PAR, chunks)):
        xh_recv(c).wait_recv()
        start(par_send(c))
        split_piece(1 + c)
    wait_recv(own_recv(0))
    wait_recv(par_recv(0))
    start(fwd_send(0))
    for i in range(1 + min(LOOK_PAR, chunks), pieces):
        split_piece(i)

    columns = (n * kdim).astype(F32)
    for b in range(2):
        found = jnp.zeros((8, kdim), F32)
        for q in range(4):
            row = jnp.broadcast_to(names[4 * b + q:4 * b + q + 1, :].astype(F32), (LANES, LANES))
            target = row.T - columns
            for t in range(kdim // LANES):
                ids = lax.broadcasted_iota(jnp.int32, (LANES, LANES), 1).astype(F32) + float(t * LANES)
                hit = jnp.where(target == ids, 1.0, 0.0)
                onehot[b, q * LANES:(q + 1) * LANES, t * LANES:(t + 1) * LANES] = hit.astype(BF16)
        total = jnp.zeros((8, kdim), F32)
        total = jnp.dot(jnp.ones((16, 4 * LANES), BF16), onehot[b], preferred_element_type=F32)
        touched[b:b + 1, :] = total[0:1, :]

    ssum[...] = jnp.zeros_like(ssum)

    @pl.when(n // 2 == s)
    def _():
        for j in range(1, NNEUR):
            other = (n + j) % NNEUR
            pltpu.make_async_remote_copy(
                src_ref=sb.at[other], dst_ref=sb.at[other], send_sem=shs_s.at[0],
                recv_sem=shs_r.at[other], device_id=(s, other), device_id_type=MESH).wait_recv()
        total = sb[0]
        for j in range(1, NNEUR):
            total = total + sb[j]
        ssum[...] = total

    in_center, in_radius = pick(ic, xl), pick(ir, xl)

    def multiply(c):
        a = g[c].reshape(16 * NSPEC, kdim)
        hi = a.astype(BF16)
        asp[0:16 * NSPEC, :] = hi
        asp[16 * NSPEC:, :] = (a - hi.astype(F32)).astype(BF16)

        def tile(j, carry):
            cols = pl.ds(pl.multiple_of(j * TILE_N, TILE_N), TILE_N)
            both = jnp.dot(asp[...], whi[:, cols], preferred_element_type=F32)
            rest = jnp.dot(asp[0:16 * NSPEC, :], wlo[:, cols], preferred_element_type=F32)
            res = both[0:16 * NSPEC] + both[16 * NSPEC:] + rest
            prod[c, :, :, :, :, cols] = res.reshape(XL, Z, 2, 8, TILE_N)
            return carry

        lax.fori_loop(0, ndim // TILE_N, tile, 0)

    def stage(cond, body):
        pl.when(cond)(body)

    def iteration(t, carry):
        @pl.when(t + LOOK_PAR < chunks)
        def _():
            c = t + LOOK_PAR
            xh_recv(c).wait_recv()
            start(par_send(c))

        @pl.when(t + LOOK_OWN < chunks)
        def _():
            start(own_send(t + LOOK_OWN))

        @pl.when(t + LOOK_XH < chunks)
        def _():
            xh_send(t + LOOK_XH).start()

        @pl.when(t + 1 < chunks)
        def _():
            wait_recv(own_recv(t + 1))
            wait_recv(par_recv(t + 1))
            start(fwd_send(t + 1))

        @pl.when(t < chunks)
        def _():
            wait_recv(fwd_recv(t))
            multiply(t)
            core_copy(t).start()

        @pl.when(jnp.logical_and(t >= 1, t - 1 < chunks))
        def _():
            c = t - 1
            wait_recv(z1_copy(c))
            for a in range(XL):
                prod[c, a, zp, k, :, 0:half] = (
                    prod[c, a, zp, k, :, 0:half] + cr[c, a, zp, :, 0:half] + z1p[c, a])
                prod[c, a, zp, k, :, half:] = prod[c, a, zp, k, :, half:] + cr[c, a, zp, :, half:]
                prod[c, a, zm, k, :, 0:half] = prod[c, a, zm, k, :, 0:half] + cr[c, a, zm, :, 0:half]
                prod[c, a, zm, k, :, half:] = (
                    prod[c, a, zm, k, :, half:] + cr[c, a, zm, :, half:] + z1m[c, a])
            start(z2_copy(c))

        @pl.when(jnp.logical_and(t >= 2, t - 2 < chunks))
        def _():
            c = t - 2
            wait_recv(z2_copy(c))
            for a in range(XL):
                prod[c, a, z, k] = prod[c, a, z, k] + cr[c, a, z] + z2p[c, a] + z2m[c, a]
            xl_copy(c).start()

        @pl.when(t >= 3)
        def _():
            c = t - 3
            xl_copy(c).wait_recv()
            v = prod[c, xl, z, k] + xb[c]
            rows = pl.ds(pl.multiple_of(c * 8, 8), 8)
            coef[rows, :] = v
            tb[rows, :] = fold_lanes(v * in_center - jnp.abs(v) * in_radius)

        @pl.when(t < chunks)
        def _():
            core_copy(t).wait_recv()
            for a in range(XL):
                prod[t, a, z2, k] = prod[t, a, z2, k] + cr[t, a, z2]
            start(z1_copy(t))

        return carry

    lax.fori_loop(0, chunks + 3, iteration, 0)

    pb[s] = rows_to_lanes(tb[...]) + ssum[...]

    def pb_copy(j, src):
        return pltpu.make_async_remote_copy(
            src_ref=pb.at[src], dst_ref=pb.at[src], send_sem=pb_s.at[j], recv_sem=pb_r.at[j],
            device_id=((s + j) % NSPEC, n), device_id_type=MESH)

    for j in range(1, NSPEC):
        pb_copy(j, s).start()
    for j in range(1, NSPEC):
        pb_copy(j, (s + NSPEC - j) % NSPEC).wait_recv()
    bound = pb[0]
    for j in range(1, NSPEC):
        bound = bound + pb[j]
    bound = bound + bias[pl.ds(n, 1), :]
    bb[n] = bound
    lbound[...] = bound[0:1, 0:lbound.shape[1]]

    def bb_copy(j, src):
        return pltpu.make_async_remote_copy(
            src_ref=bb.at[src], dst_ref=bb.at[src], send_sem=bb_s.at[j], recv_sem=bb_r.at[j],
            device_id=(s, (n + j) % NNEUR), device_id_type=MESH)

    for j in range(1, NNEUR):
        bb_copy(j, n).start()

    def drain(c, carry):
        xh_send(c).wait_send()
        core_copy(c).wait_send()
        xl_copy(c).wait_send()
        for copies in (own_send(c), par_send(c), fwd_send(c), z1_copy(c), z2_copy(c)):
            for copy in copies:
                copy.wait_send()
        return carry

    lax.fori_loop(0, chunks, drain, 0)
    for h in range(2):
        @pl.when(n != 2 * s + h)
        def _(h=h):
            shs_copy(h).wait_send()

    for j in range(1, NNEUR):
        bb_copy(j, (n + NNEUR - j) % NNEUR).wait_recv()

    row = lax.broadcasted_iota(jnp.int32, (8, 4 * LANES), 0)

    def parts(first):
        v = jnp.concatenate([bb[first + i] for i in range(4)], axis=1)
        p1 = v.astype(BF16).astype(F32)
        p2 = (v - p1).astype(BF16).astype(F32)
        p3 = v - p1 - p2
        return jnp.where(row == 0, p1, jnp.where(row == 1, p2, jnp.where(row == 2, p3, 0.0)))

    for b in range(2):
        lhs = jnp.concatenate([parts(8 * b), parts(8 * b + 4)], axis=0).astype(BF16)
        picked = jnp.dot(lhs, onehot[b], preferred_element_type=F32)
        low_found = jnp.sum(picked[0:8], axis=0, keepdims=True)
        high_found = -jnp.sum(picked[8:16], axis=0, keepdims=True)
        hit = touched[b:b + 1, :] > 0.0
        low0, high0 = plow[b:b + 1, :], phigh[b:b + 1, :]
        new_low = jnp.where(hit, jnp.maximum(low0, low_found), low0)
        new_high = jnp.where(hit, jnp.minimum(high0, high_found), high0)
        rising, falling = jnp.maximum(new_high, 0.0), jnp.maximum(-new_low, 0.0)
        unstable = jnp.logical_and(new_low < 0.0, new_high > 0.0)
        safe = jnp.where(unstable, rising + falling, 1.0)
        slope = jnp.where(new_low >= 0.0, 1.0, jnp.where(new_high <= 0.0, 0.0, rising / safe))
        nslope[b:b + 1, :] = slope
        nshift[b:b + 1, :] = slope * falling

    for j in range(1, NSPEC):
        pb_copy(j, s).wait_send()
    for j in range(1, NNEUR):
        bb_copy(j, n).wait_send()


def per_device(panel, weight, layer_bias, act_center, act_radius, alpha, in_center, in_radius,
               bias_in, spec_neuron, prior_lower, prior_upper):
    own_rows, kdim = panel.shape
    ndim = weight.shape[1]
    hrows = own_rows // 2
    chunks = hrows // 8
    spec_rows = bias_in.shape[0] // NNEUR
    names = jnp.pad(spec_neuron.reshape(8, -1), ((0, 0), (0, LANES - spec_rows)), constant_values=-1)
    bias = jnp.pad(bias_in.reshape(NNEUR, spec_rows), ((0, 0), (0, LANES - spec_rows)))
    vmem = pl.BlockSpec(memory_space=pltpu.VMEM)
    hbm = pl.BlockSpec(memory_space=pl.ANY)
    half = ndim // 2
    dma = pltpu.SemaphoreType.DMA
    coef, lbound, nslope, nshift = pl.pallas_call(
        kernel,
        out_shape=(
            jax.ShapeDtypeStruct((hrows, ndim), F32),
            jax.ShapeDtypeStruct((1, spec_rows), F32),
            jax.ShapeDtypeStruct((2, kdim), F32),
            jax.ShapeDtypeStruct((2, kdim), F32),
        ),
        in_specs=[hbm, hbm] + [vmem] * 10,
        out_specs=(vmem,) * 4,
        scratch_shapes=[
            pltpu.VMEM((2, hrows, kdim), F32),
            pltpu.VMEM((kdim // W_ROWS, W_ROWS, ndim), F32),
            pltpu.VMEM((kdim, ndim), BF16),
            pltpu.VMEM((kdim, ndim), BF16),
            pltpu.VMEM((chunks, XH, Y, 2, 8, kdim), F32),
            pltpu.VMEM((2 * 16 * NSPEC, kdim), BF16),
            pltpu.VMEM((chunks, XL, Z, 2, 8, ndim), F32),
            pltpu.VMEM((chunks, XL, Z, 8, ndim), F32),
            pltpu.VMEM((chunks, XL, 8, half), F32),
            pltpu.VMEM((chunks, XL, 8, half), F32),
            pltpu.VMEM((chunks, XL, 8, ndim), F32),
            pltpu.VMEM((chunks, XL, 8, ndim), F32),
            pltpu.VMEM((chunks, 8, ndim), F32),
            pltpu.VMEM((2, LANES, LANES), F32),
            pltpu.VMEM((LANES, LANES), F32),
            pltpu.VMEM((2, 8, LANES), F32),
            pltpu.VMEM((NNEUR, 8, LANES), F32),
            pltpu.VMEM((8, LANES), F32),
            pltpu.VMEM((NSPEC, 8, LANES), F32),
            pltpu.VMEM((NNEUR, 8, LANES), F32),
            pltpu.VMEM((2, 4 * LANES, kdim), BF16),
            pltpu.VMEM((2, kdim), F32),
            dma((1 + kdim // W_ROWS,)),
            dma((chunks, NCOPY)), dma((chunks, NCOPY)),
            dma((2,)), dma((NNEUR,)),
            dma((NSPEC,)), dma((NSPEC,)),
            dma((NNEUR,)), dma((NNEUR,)),
        ],
        compiler_params=pltpu.CompilerParams(
            collective_id=0, has_side_effects=True, vmem_limit_bytes=60 * 1024 * 1024),
        cost_estimate=pl.CostEstimate(
            flops=6 * 8 * own_rows * kdim * ndim, bytes_accessed=4 * kdim * ndim, transcendentals=0),
    )(panel.reshape(2, hrows, kdim), weight, layer_bias.reshape(1, kdim), act_center, act_radius,
      alpha, in_center, in_radius, bias, names, prior_lower, prior_upper)
    return coef, lbound.reshape(spec_rows), nslope, nshift


def solution(mesh):
    in_specs = (
        P("spec", "neuron"),
        P("neuron", "spec"),
        P("neuron"),
        P(None, "neuron"),
        P(None, "neuron"),
        P(None, "neuron"),
        P(None, "spec"),
        P(None, "spec"),
        P(),
        P(),
        P(None, "neuron"),
        P(None, "neuron"),
    )
    out_specs = (P("neuron", "spec"), P("neuron"), P(None, "neuron"), P(None, "neuron"))
    return jax.shard_map(
        per_device, mesh=mesh, in_specs=in_specs, out_specs=out_specs, check_vma=False
    )
```

time: 348 us -> 128 us (0.37); the launches traced: 343 us -> 128 us
  waiting for transfers between devices: 217 us -> 0 us
  Pallas kernels: 0 us -> 119 us
  blocking collectives: 48.5 us -> 0 us
  matrix products: 46.2 us -> 0 us
  between operations: 14.9 us -> 0.64 us
  other arithmetic: 12.2 us -> 0 us
  local copies, waits for them, and re-layouts: 4.39 us -> 8.56 us
    psum x1 -> x0, waiting for transfers between devices: 125 us -> none  [per_device(): product = lax.psum(product, 'neuron')]
    pallas_call x0 -> x1, Pallas kernels: none -> 119 us  [per_device(): pl.pallas_call(kernel, out_shape=(jax.ShapeDtypeStruct((hrows, ndim), F32...]
    all_gather x1 -> x0, waiting for transfers between devices: 92 us -> none  [per_device(): lax.all_gather(relaxed, 'spec', axis=0, tiled=True)]
    psum x2 -> x0, blocking collectives: 48.5 us -> none  [the longest x1 28 us: per_device(): shift_rows = lax.psum(shift_local, 'neuron')]
    dot_general x2 -> x0, matrix products: 46.2 us -> none  [the longest x1 45.5 us: per_device(): jnp.dot(gathered, weight, precision=lax.Precision.HIGHEST, preferred_elem...]
    reduce_sum x3 -> x0, other arithmetic: 10 us -> none  [the longest x1 7.04 us: concretize(): jnp.sum(coefs * pick_rows(center, row_sample) - jnp.abs(coefs) * pick_row...]
    unnamed x21 -> x4, local copies, waits for them, and re-layouts: 1.67 us -> 5.83 us
  transfers between devices with their start and end apart: 2 -> 0, of which waited for: 2 -> 0; matrix products, arithmetic and copies ran while one was open for 1% -> 0% of each run, Pallas kernels for 0% -> 0%
where the time goes in v1:
time: 128 us
  Pallas kernels  119 us (93%)
  local copies, waits for them, and re-layouts  8.56 us (7%)
    pallas_call x1, Pallas kernels, per_device(): pl.pallas_call(kernel, out_shape=(jax.ShapeDtypeStruct((hrows, ndim), F32...  119 us
    unnamed x4, local copies, waits for them, and re-layouts  5.83 us

profile of v1, /device:TPU:1, one launch (start us, length us, event | category | flops | bytes accessed | tf_op | source)
XLA Modules:
  0.0 127.9 jit_solution(10696298904905758236)
XLA Ops:
  0.6 0.8 reshape.26
  1.4 0.6 pad.9.names
  2.0 0.8 reshape.25
  2.8 0.6 pad.8.bias
  3.4 118.7 %shard_map.147 = (f32[96,2048]{1,0:T(8,128)}, f32[1,96]{1,0:T(1,128)}, f32[2,1024]{1,0:T(2,128)}, f32[2,1024]{1,0:T(2,128)}) custom-call(f32[2,96,1024]{2,1,0:T(8,128)} %bitcast.3, f32[1024,2048]{1,0:T(8,128)} %weight.1, f32[1,1024]{1,0:T(1,128)} %bitcast.4, f32[2,1024]{1,0:T(2,128)} %ac.1, f32[2,1024]{1,0:T(2,128)} %ar.1, f32[2,1024]{1,0:T(2,128)} %al.1, ...), custom_call_target="tpu_custom_call" | custom-call | flops 19327352832 | bytes 8388608 | tf_op jit(solution)/shard_map/pallas_call | solution.py:409
  122.0 2.1 %copy.20 = f32[96,2048]{1,0:T(8,128)} copy(f32[96,2048]{1,0:T(8,128)} %get-tuple-element.16) | data formatting | bytes 1572864
  124.1 1.2 copy.21
  125.3 1.3 %copy.22 = f32[2,1024]{1,0:T(2,128)} copy(f32[2,1024]{1,0:T(2,128)} %get-tuple-element.18) | data formatting | bytes 16384
  126.6 1.3 %copy.23 = f32[2,1024]{1,0:T(2,128)} copy(f32[2,1024]{1,0:T(2,128)} %get-tuple-element.19) | data formatting | bytes 16384

commit v2 on v1

--- a/solution.py
+++ b/solution.py
@@ -14,12 +14,14 @@
 NSPEC, NNEUR = XH * Y, XL * Z * 2
 LANES = 128
 
-(S_XH, S_OWN_P, S_OWN_M, S_PAR_P, S_PAR_M, S_F0_P, S_F1_P, S_F0_M, S_F1_M,
- S_CORE, S_Z1_P, S_Z1_M, S_Z2_P, S_Z2_M, S_XL) = range(15)
-NCOPY = 15
-
+(S_XH, S_OWN_P, S_OWN_M, S_PAR_P, S_PAR_M, S_FWD_P, S_FWD_M,
+ S_CORE, S_Z1_P, S_Z1_M, S_Z2_P, S_Z2_M, S_XL) = range(13)
+NCOPY = 13
+
+LAG_Z2 = 2
+LAG_FIN = 4
+LAG_OUT = 5
 LOOK_XH = 4
-LOOK_OWN = 3
 LOOK_PAR = 2
 TILE_N = 512
 W_ROWS = 256
@@ -38,11 +40,18 @@
         precision=lax.Precision.HIGHEST, preferred_element_type=F32)
 
 
-def kernel(panel, weight, lbias, ac, ar, al, ic, ir, bias, names, plow, phigh,
-           coef, lbound, nslope, nshift,
+def kernel(panel, weight, *rest):
+    small_in = rest[:10]
+    coef = rest[10]
+    lbound, nslope, nshift = rest[11:14]
+    small = rest[14:24]
+    body(panel, weight, small_in, small, coef, lbound, nslope, nshift, *rest[24:])
+
+
+def body(panel, weight, small_in, small, coef, lbound, nslope, nshift,
            pan, wst, whi, wlo, g, asp, prod, cr, z1p, z1m, z2p, z2m, xb,
-           ts, tb, shs, sb, ssum, pb, bb, onehot, touched,
-           dsem, ssem, rsem, shs_s, shs_r, pb_s, pb_r, bb_s, bb_r):
+           ts, tb, shs, sb, pb, bb, onehot, touched, bias16, out,
+           dsem, osem, ssem, rsem, shs_s, shs_r, pb_s, pb_r, bb_s, bb_r):
     chunks = g.shape[0]
     kdim, ndim = whi.shape
     half = ndim // 2
@@ -59,20 +68,29 @@
     dev_zp, dev_zm = (s, xl * 2 * Z + zp * 2 + k), (s, xl * 2 * Z + zm * 2 + k)
     dev_xl = (s, (1 - xl) * 2 * Z + z * 2 + k)
 
-    load_panel = pltpu.make_async_copy(panel, pan, dsem.at[0])
-    load_panel.start()
-    pieces = kdim // W_ROWS
-    w_loads = [
-        pltpu.make_async_copy(weight.at[pl.ds(i * W_ROWS, W_ROWS)], wst.at[i], dsem.at[1 + i])
-        for i in range(pieces)]
-    for w_load in w_loads:
-        w_load.start()
-
     barrier = pltpu.get_barrier_semaphore()
     for j in range(1, NSPEC):
         pl.semaphore_signal(barrier, inc=1, device_id=((s + j) % NSPEC, n), device_id_type=MESH)
     for j in range(1, NNEUR):
         pl.semaphore_signal(barrier, inc=1, device_id=(s, (n + j) % NNEUR), device_id_type=MESH)
+
+    loads = [pltpu.make_async_copy(a, b, dsem.at[i]) for i, (a, b) in enumerate(zip(small_in, small))]
+    load_panel = pltpu.make_async_copy(panel, pan, dsem.at[10])
+    for load in loads[:4]:
+        load.start()
+    load_panel.start()
+    for load in loads[4:]:
+        load.start()
+    pieces = kdim // W_ROWS
+    w_loads = [
+        pltpu.make_async_copy(weight.at[pl.ds(i * W_ROWS, W_ROWS)], wst.at[i], dsem.at[11 + i])
+        for i in range(pieces)]
+    for w_load in w_loads:
+        w_load.start()
+    lbias, ac, ar, al, ic, ir, bias, names, plow, phigh = small
+
+    for load in loads[:4]:
+        load.wait()
 
     def pick(ref, i):
         return jnp.where(i == 0, ref[0:1, :], ref[1:2, :])
@@ -97,7 +115,8 @@
             ts[h, pl.ds(pl.multiple_of(c * 8, 8), 8), :] = fold_lanes(rel * lb + neg * up_shift)
         return carry
 
-    lax.fori_loop(0, chunks, relax, 0)
+    first = min(LOOK_PAR, chunks)
+    lax.fori_loop(0, first, relax, 0)
     pl.semaphore_wait(barrier, NSPEC + NNEUR - 2)
 
     def rc(src, dst, kind, c, dev):
@@ -108,8 +127,11 @@
     def block_copy(kind, c, bx, by, dev):
         return rc(g.at[c, bx, by], g.at[c, bx, by], kind, c, dev)
 
-    def half_copy(kind, c, bx, by, h, dev):
-        return rc(g.at[c, bx, by, h], g.at[c, bx, by, h], kind, c, dev)
+    def pair_copy(kind, c, by, dev):
+        return rc(g.at[c, :, by], g.at[c, :, by], kind, c, dev)
+
+    def half_copy(kind, c, by, h, dev):
+        return rc(g.at[c, :, by, h], g.at[c, :, by, h], kind, c, dev)
 
     def xh_send(c): return block_copy(S_XH, c, xh, y, dev_xh)
     def xh_recv(c): return block_copy(S_XH, c, 1 - xh, y, dev_xh)
@@ -126,13 +148,17 @@
     def par_recv(c):
         return [block_copy(S_PAR_P, c, 1 - xh, ym, dev_yp), block_copy(S_PAR_M, c, 1 - xh, yp, dev_ym)]
 
+    def pair_send(c):
+        return [pair_copy(S_OWN_P, c, y, dev_yp), pair_copy(S_OWN_M, c, y, dev_ym)]
+
+    def pair_recv(c):
+        return [pair_copy(S_OWN_P, c, ym, dev_yp), pair_copy(S_OWN_M, c, yp, dev_ym)]
+
     def fwd_send(c):
-        return [half_copy(S_F0_P, c, xh, ym, 0, dev_yp), half_copy(S_F0_M, c, xh, yp, 1, dev_ym),
-                half_copy(S_F1_P, c, 1 - xh, ym, 0, dev_yp), half_copy(S_F1_M, c, 1 - xh, yp, 1, dev_ym)]
+        return [half_copy(S_FWD_P, c, ym, 0, dev_yp), half_copy(S_FWD_M, c, yp, 1, dev_ym)]
 
     def fwd_recv(c):
-        return [half_copy(S_F0_P, c, xh, y2, 0, dev_yp), half_copy(S_F0_M, c, xh, y2, 1, dev_ym),
-                half_copy(S_F1_P, c, 1 - xh, y2, 0, dev_yp), half_copy(S_F1_M, c, 1 - xh, y2, 1, dev_ym)]
+        return [half_copy(S_FWD_P, c, y2, 0, dev_yp), half_copy(S_FWD_M, c, y2, 1, dev_ym)]
 
     def core_copy(c):
         return rc(prod.at[c, :, :, 1 - k], cr.at[c], S_CORE, c, dev_core)
@@ -148,6 +174,10 @@
     def xl_copy(c):
         return rc(prod.at[c, 1 - xl, z, k], xb.at[c], S_XL, c, dev_xl)
 
+    def out_copy(c):
+        return pltpu.make_async_copy(
+            out.at[c], coef.at[pl.ds(pl.multiple_of(c * 8, 8), 8)], osem.at[c])
+
     def start(copies):
         for copy in copies:
             copy.start()
@@ -156,10 +186,11 @@
         for copy in copies:
             copy.wait_recv()
 
-    for c in range(min(LOOK_OWN, chunks)):
+    for c in range(first):
         xh_send(c).start()
         start(own_send(c))
-    for c in range(LOOK_OWN, min(LOOK_XH, chunks)):
+    lax.fori_loop(first, chunks, relax, 0)
+    for c in range(LOOK_PAR, min(LOOK_XH, chunks)):
         xh_send(c).start()
 
     for h in range(2):
@@ -201,35 +232,45 @@
     for i in range(1 + min(LOOK_PAR, chunks), pieces):
         split_piece(i)
 
+    for load in loads[4:]:
+        load.wait()
+
+    def row_piece(v, first, count):
+        at = first // LANES * LANES
+        if first % LANES == 0:
+            return v[:, at:at + LANES]
+        width = min(2 * LANES, v.shape[1] - at)
+        return pltpu.roll(v[:, at:at + width], width - first % LANES, 1)[:, 0:LANES]
+
+    spec_rows = lbound.shape[1]
+    lane = lax.broadcasted_iota(jnp.int32, (1, LANES), 1)
+    bias_row = jnp.concatenate([bias[i:i + 1, :] for i in range(bias.shape[0])], axis=1)
+    for j in range(NNEUR):
+        piece = row_piece(bias_row, j * spec_rows, spec_rows)
+        bias16[j:j + 1, :] = jnp.where(lane < spec_rows, piece, 0.0)
     columns = (n * kdim).astype(F32)
     for b in range(2):
-        found = jnp.zeros((8, kdim), F32)
         for q in range(4):
-            row = jnp.broadcast_to(names[4 * b + q:4 * b + q + 1, :].astype(F32), (LANES, LANES))
+            row = row_piece(names[b:b + 1, :].astype(F32), q * spec_rows, spec_rows)
+            row = jnp.broadcast_to(jnp.where(lane < spec_rows, row, -1.0), (LANES, LANES))
             target = row.T - columns
             for t in range(kdim // LANES):
                 ids = lax.broadcasted_iota(jnp.int32, (LANES, LANES), 1).astype(F32) + float(t * LANES)
                 hit = jnp.where(target == ids, 1.0, 0.0)
                 onehot[b, q * LANES:(q + 1) * LANES, t * LANES:(t + 1) * LANES] = hit.astype(BF16)
-        total = jnp.zeros((8, kdim), F32)
         total = jnp.dot(jnp.ones((16, 4 * LANES), BF16), onehot[b], preferred_element_type=F32)
         touched[b:b + 1, :] = total[0:1, :]
 
-    ssum[...] = jnp.zeros_like(ssum)
-
-    @pl.when(n // 2 == s)
-    def _():
+    def shift_recv():
         for j in range(1, NNEUR):
             other = (n + j) % NNEUR
             pltpu.make_async_remote_copy(
                 src_ref=sb.at[other], dst_ref=sb.at[other], send_sem=shs_s.at[0],
                 recv_sem=shs_r.at[other], device_id=(s, other), device_id_type=MESH).wait_recv()
-        total = sb[0]
-        for j in range(1, NNEUR):
-            total = total + sb[j]
-        ssum[...] = total
 
     in_center, in_radius = pick(ic, xl), pick(ir, xl)
+    row8 = lax.broadcasted_iota(jnp.int32, (8, LANES), 0)
+    lane8 = lax.broadcasted_iota(jnp.int32, (8, LANES), 1)
 
     def multiply(c):
         a = g[c].reshape(16 * NSPEC, kdim)
@@ -250,25 +291,47 @@
     def stage(cond, body):
         pl.when(cond)(body)
 
+    def drain(c):
+        xh_send(c).wait_send()
+        core_copy(c).wait_send()
+        xl_copy(c).wait_send()
+        out_copy(c).wait()
+        for copies in (fwd_send(c), z1_copy(c), z2_copy(c)):
+            for copy in copies:
+                copy.wait_send()
+
+        @pl.when(c < LOOK_PAR)
+        def _():
+            for copy in own_send(c) + par_send(c):
+                copy.wait_send()
+
+        @pl.when(c >= LOOK_PAR)
+        def _():
+            for copy in pair_send(c):
+                copy.wait_send()
+
     def iteration(t, carry):
         @pl.when(t + LOOK_PAR < chunks)
         def _():
             c = t + LOOK_PAR
             xh_recv(c).wait_recv()
-            start(par_send(c))
-
-        @pl.when(t + LOOK_OWN < chunks)
-        def _():
-            start(own_send(t + LOOK_OWN))
+            start(pair_send(c))
 
         @pl.when(t + LOOK_XH < chunks)
         def _():
             xh_send(t + LOOK_XH).start()
 
-        @pl.when(t + 1 < chunks)
+        @pl.when(t + 1 < LOOK_PAR)
         def _():
             wait_recv(own_recv(t + 1))
             wait_recv(par_recv(t + 1))
+
+        @pl.when(jnp.logical_and(t + 1 >= LOOK_PAR, t + 1 < chunks))
+        def _():
+            wait_recv(pair_recv(t + 1))
+
+        @pl.when(t + 1 < chunks)
+        def _():
             start(fwd_send(t + 1))
 
         @pl.when(t < chunks)
@@ -280,6 +343,14 @@
         @pl.when(jnp.logical_and(t >= 1, t - 1 < chunks))
         def _():
             c = t - 1
+            core_copy(c).wait_recv()
+            for a in range(XL):
+                prod[c, a, z2, k] = prod[c, a, z2, k] + cr[c, a, z2]
+            start(z1_copy(c))
+
+        @pl.when(jnp.logical_and(t >= LAG_Z2, t - LAG_Z2 < chunks))
+        def _():
+            c = t - LAG_Z2
             wait_recv(z1_copy(c))
             for a in range(XL):
                 prod[c, a, zp, k, :, 0:half] = (
@@ -290,35 +361,41 @@
                     prod[c, a, zm, k, :, half:] + cr[c, a, zm, :, half:] + z1m[c, a])
             start(z2_copy(c))
 
-        @pl.when(jnp.logical_and(t >= 2, t - 2 < chunks))
-        def _():
-            c = t - 2
+        @pl.when(jnp.logical_and(t >= LAG_FIN, t - LAG_FIN < chunks))
+        def _():
+            c = t - LAG_FIN
             wait_recv(z2_copy(c))
             for a in range(XL):
                 prod[c, a, z, k] = prod[c, a, z, k] + cr[c, a, z] + z2p[c, a] + z2m[c, a]
             xl_copy(c).start()
 
-        @pl.when(t >= 3)
-        def _():
-            c = t - 3
+        @pl.when(t > LAG_OUT)
+        def _():
+            drain(t - LAG_OUT - 1)
+
+        @pl.when(t >= LAG_OUT)
+        def _():
+            c = t - LAG_OUT
             xl_copy(c).wait_recv()
             v = prod[c, xl, z, k] + xb[c]
-            rows = pl.ds(pl.multiple_of(c * 8, 8), 8)
-            coef[rows, :] = v
-            tb[rows, :] = fold_lanes(v * in_center - jnp.abs(v) * in_radius)
-
-        @pl.when(t < chunks)
-        def _():
-            core_copy(t).wait_recv()
-            for a in range(XL):
-                prod[t, a, z2, k] = prod[t, a, z2, k] + cr[t, a, z2]
-            start(z1_copy(t))
+            out[c] = v
+            out_copy(c).start()
+            total = jnp.sum(fold_lanes(v * in_center - jnp.abs(v) * in_radius), axis=1, keepdims=True)
+            tb[...] += jnp.where(lane8 == row8 + c * 8, jnp.broadcast_to(total, (8, LANES)), 0.0)
+
+        @pl.when(jnp.logical_and(t == 2, n // 2 == s))
+        def _():
+            shift_recv()
+            total = sb[0]
+            for j in range(1, NNEUR):
+                total = total + sb[j]
+            tb[...] += jnp.where(row8 == 0, total + bias16[pl.ds(n, 1), :], 0.0)
 
         return carry
 
-    lax.fori_loop(0, chunks + 3, iteration, 0)
-
-    pb[s] = rows_to_lanes(tb[...]) + ssum[...]
+    lax.fori_loop(0, chunks + LAG_OUT, iteration, 0)
+
+    pb[s] = tb[...]
 
     def pb_copy(j, src):
         return pltpu.make_async_remote_copy(
@@ -332,7 +409,7 @@
     bound = pb[0]
     for j in range(1, NSPEC):
         bound = bound + pb[j]
-    bound = bound + bias[pl.ds(n, 1), :]
+    bound = jnp.broadcast_to(jnp.sum(bound, axis=0, keepdims=True), (8, LANES))
     bb[n] = bound
     lbound[...] = bound[0:1, 0:lbound.shape[1]]
 
@@ -344,16 +421,7 @@
     for j in range(1, NNEUR):
         bb_copy(j, n).start()
 
-    def drain(c, carry):
-        xh_send(c).wait_send()
-        core_copy(c).wait_send()
-        xl_copy(c).wait_send()
-        for copies in (own_send(c), par_send(c), fwd_send(c), z1_copy(c), z2_copy(c)):
-            for copy in copies:
-                copy.wait_send()
-        return carry
-
-    lax.fori_loop(0, chunks, drain, 0)
+    drain(chunks - 1)
     for h in range(2):
         @pl.when(n != 2 * s + h)
         def _(h=h):
@@ -400,13 +468,13 @@
     hrows = own_rows // 2
     chunks = hrows // 8
     spec_rows = bias_in.shape[0] // NNEUR
-    names = jnp.pad(spec_neuron.reshape(8, -1), ((0, 0), (0, LANES - spec_rows)), constant_values=-1)
-    bias = jnp.pad(bias_in.reshape(NNEUR, spec_rows), ((0, 0), (0, LANES - spec_rows)))
     vmem = pl.BlockSpec(memory_space=pltpu.VMEM)
     hbm = pl.BlockSpec(memory_space=pl.ANY)
     half = ndim // 2
     dma = pltpu.SemaphoreType.DMA
-    coef, lbound, nslope, nshift = pl.pallas_call(
+    small_in = (layer_bias.reshape(1, kdim), act_center, act_radius, alpha, in_center, in_radius,
+                bias_in.reshape(-1, LANES), spec_neuron, prior_lower, prior_upper)
+    results = pl.pallas_call(
         kernel,
         out_shape=(
             jax.ShapeDtypeStruct((hrows, ndim), F32),
@@ -414,9 +482,9 @@
             jax.ShapeDtypeStruct((2, kdim), F32),
             jax.ShapeDtypeStruct((2, kdim), F32),
         ),
-        in_specs=[hbm, hbm] + [vmem] * 10,
-        out_specs=(vmem,) * 4,
-        scratch_shapes=[
+        in_specs=[hbm] * 12,
+        out_specs=(hbm, vmem, vmem, vmem),
+        scratch_shapes=[pltpu.VMEM(a.shape, a.dtype) for a in small_in] + [
             pltpu.VMEM((2, hrows, kdim), F32),
             pltpu.VMEM((kdim // W_ROWS, W_ROWS, ndim), F32),
             pltpu.VMEM((kdim, ndim), BF16),
@@ -431,15 +499,16 @@
             pltpu.VMEM((chunks, XL, 8, ndim), F32),
             pltpu.VMEM((chunks, 8, ndim), F32),
             pltpu.VMEM((2, LANES, LANES), F32),
-            pltpu.VMEM((LANES, LANES), F32),
+            pltpu.VMEM((8, LANES), F32),
             pltpu.VMEM((2, 8, LANES), F32),
             pltpu.VMEM((NNEUR, 8, LANES), F32),
-            pltpu.VMEM((8, LANES), F32),
             pltpu.VMEM((NSPEC, 8, LANES), F32),
             pltpu.VMEM((NNEUR, 8, LANES), F32),
             pltpu.VMEM((2, 4 * LANES, kdim), BF16),
             pltpu.VMEM((2, kdim), F32),
-            dma((1 + kdim // W_ROWS,)),
+            pltpu.VMEM((NNEUR, LANES), F32),
+            pltpu.VMEM((chunks, 8, ndim), F32),
+            dma((11 + kdim // W_ROWS,)), dma((chunks,)),
             dma((chunks, NCOPY)), dma((chunks, NCOPY)),
             dma((2,)), dma((NNEUR,)),
             dma((NSPEC,)), dma((NSPEC,)),
@@ -449,9 +518,44 @@
             collective_id=0, has_side_effects=True, vmem_limit_bytes=60 * 1024 * 1024),
         cost_estimate=pl.CostEstimate(
             flops=6 * 8 * own_rows * kdim * ndim, bytes_accessed=4 * kdim * ndim, transcendentals=0),
-    )(panel.reshape(2, hrows, kdim), weight, layer_bias.reshape(1, kdim), act_center, act_radius,
-      alpha, in_center, in_radius, bias, names, prior_lower, prior_upper)
+    )(panel.reshape(2, hrows, kdim), weight, *small_in)
+    coef, lbound, nslope, nshift = hand_on(results)
     return coef, lbound.reshape(spec_rows), nslope, nshift
+
+
+def hand_on(arrays):
+    count = len(arrays)
+    parts = 6
+    step = arrays[0].shape[0] // parts
+
+    def copy_kernel(*refs):
+        held = refs[2 * count:3 * count]
+        sems_in, sems_out = refs[3 * count:]
+
+        def moves(source, target, sems):
+            pairs = [(source[0].at[pl.ds(i * step, step)], target[0].at[pl.ds(i * step, step)])
+                     for i in range(parts)]
+            pairs += [(source[i], target[i]) for i in range(1, count)]
+            return [pltpu.make_async_copy(a, b, sems.at[i]) for i, (a, b) in enumerate(pairs)]
+
+        into, outof = moves(refs[:count], held, sems_in), moves(held, refs[count:2 * count], sems_out)
+        for copy in into:
+            copy.start()
+        for first, second in zip(into, outof):
+            first.wait()
+            second.start()
+        for copy in outof:
+            copy.wait()
+
+    hbm = pl.BlockSpec(memory_space=pl.ANY)
+    return pl.pallas_call(
+        copy_kernel,
+        out_shape=tuple(jax.ShapeDtypeStruct(a.shape, a.dtype) for a in arrays),
+        in_specs=[hbm] * count,
+        out_specs=(hbm,) * count,
+        scratch_shapes=[pltpu.VMEM(a.shape, a.dtype) for a in arrays]
+        + [pltpu.SemaphoreType.DMA((parts + count,))] * 2,
+    )(*arrays)
 
 
 def solution(mesh):

time: 128 us -> 104 us (0.81)
  Pallas kernels: 119 us -> 103 us
  local copies, waits for them, and re-layouts: 8.56 us -> 0 us
    pallas_call x1, Pallas kernels: 119 us -> 101 us  [per_device(): pl.pallas_call(kernel, out_shape=(jax.ShapeDtypeStruct((hrows, ndim), F32...]
    unnamed x4 -> x0, local copies, waits for them, and re-layouts: 5.83 us -> none
    pallas_call x0 -> x1, Pallas kernels: none -> 2.04 us  [hand_on(): pl.pallas_call(copy_kernel, out_shape=tuple((jax.ShapeDtypeStruct(a.shape...]
    reshape x2 -> x0, local copies, waits for them, and re-layouts: 1.53 us -> none  [the longest x1 0.77 us: per_device(): bias_in.reshape(NNEUR, spec_rows)]
where the time goes in v2:
time: 104 us
  Pallas kernels  103 us (99%)
    pallas_call x1, Pallas kernels, per_device(): pl.pallas_call(kernel, out_shape=(jax.ShapeDtypeStruct((hrows, ndim), F32...  101 us

profile of v2, /device:TPU:1, one launch (start us, length us, event | category | flops | bytes accessed | tf_op | source)
XLA Modules:
  0.0 103.9 jit_solution(8610000781454865700)
XLA Ops:
  0.6 101.2 %shard_map.147 = (f32[96,2048]{1,0:T(8,128)}, f32[1,96]{1,0:T(1,128)}, f32[2,1024]{1,0:T(2,128)}, f32[2,1024]{1,0:T(2,128)}) custom-call(f32[2,96,1024]{2,1,0:T(8,128)} %bitcast.4, f32[1024,2048]{1,0:T(8,128)} %weight.1, f32[1,1024]{1,0:T(1,128)} %bitcast.6, f32[2,1024]{1,0:T(2,128)} %rest_1_.1, f32[2,1024]{1,0:T(2,128)} %rest_2_.1, f32[2,1024]{1,0:T(2,128)} %rest_3_.1, ...), custom_call_target="tpu_custom_call" | custom-call | flops 19327352832 | bytes 8388608 | tf_op jit(solution)/shard_map/pallas_call | solution.py:477
  101.8 2.0 %shard_map.148 = (f32[96,2048]{1,0:T(8,128)}, f32[1,96]{1,0:T(1,128)}, f32[2,1024]{1,0:T(2,128)}, f32[2,1024]{1,0:T(2,128)}) custom-call(f32[96,2048]{1,0:T(8,128)} %get-tuple-element.12.refs_0_, f32[1,96]{1,0:T(1,128)} %get-tuple-element.13.refs_1_, f32[2,1024]{1,0:T(2,128)} %get-tuple-element.14.refs_2_, f32[2,1024]{1,0:T(2,128)} %get-tuple-element.15.refs_3_), custom_call_target="tpu_custom_call" | custom-call | tf_op jit(solution)/shard_map/pallas_call | solution.py:551

commit v3 on v2

--- a/solution.py
+++ b/solution.py
@@ -14,16 +14,16 @@
 NSPEC, NNEUR = XH * Y, XL * Z * 2
 LANES = 128
 
-(S_XH, S_OWN_P, S_OWN_M, S_PAR_P, S_PAR_M, S_FWD_P, S_FWD_M,
- S_CORE, S_Z1_P, S_Z1_M, S_Z2_P, S_Z2_M, S_XL) = range(13)
-NCOPY = 13
+(S_XH, S_OWN_P, S_OWN_M, S_PAR_P, S_PAR_M, S_PAIR_P, S_PAIR_M, S_FWD_P, S_FWD_M,
+ S_CORE, S_Z1_P, S_Z1_M, S_Z2_P, S_Z2_M, S_XL) = range(15)
+NCOPY = 15
 
 LAG_Z2 = 2
 LAG_FIN = 4
 LAG_OUT = 5
 LOOK_XH = 4
 LOOK_PAR = 2
-TILE_N = 512
+TILE_N = 1024
 W_ROWS = 256
 
 
@@ -69,10 +69,9 @@
     dev_xl = (s, (1 - xl) * 2 * Z + z * 2 + k)
 
     barrier = pltpu.get_barrier_semaphore()
-    for j in range(1, NSPEC):
-        pl.semaphore_signal(barrier, inc=1, device_id=((s + j) % NSPEC, n), device_id_type=MESH)
-    for j in range(1, NNEUR):
-        pl.semaphore_signal(barrier, inc=1, device_id=(s, (n + j) % NNEUR), device_id_type=MESH)
+    near = (dev_xh, dev_yp, dev_ym, dev_core, dev_zp, dev_zm, dev_xl)
+    for dev in near:
+        pl.semaphore_signal(barrier, inc=1, device_id=dev, device_id_type=MESH)
 
     loads = [pltpu.make_async_copy(a, b, dsem.at[i]) for i, (a, b) in enumerate(zip(small_in, small))]
     load_panel = pltpu.make_async_copy(panel, pan, dsem.at[10])
@@ -117,11 +116,11 @@
 
     first = min(LOOK_PAR, chunks)
     lax.fori_loop(0, first, relax, 0)
-    pl.semaphore_wait(barrier, NSPEC + NNEUR - 2)
+    pl.semaphore_wait(barrier, len(near))
 
     def rc(src, dst, kind, c, dev):
         return pltpu.make_async_remote_copy(
-            src_ref=src, dst_ref=dst, send_sem=ssem.at[c, kind], recv_sem=rsem.at[c, kind],
+            src_ref=src, dst_ref=dst, send_sem=ssem.at[kind], recv_sem=rsem.at[c, kind],
             device_id=dev, device_id_type=MESH)
 
     def block_copy(kind, c, bx, by, dev):
@@ -149,10 +148,10 @@
         return [block_copy(S_PAR_P, c, 1 - xh, ym, dev_yp), block_copy(S_PAR_M, c, 1 - xh, yp, dev_ym)]
 
     def pair_send(c):
-        return [pair_copy(S_OWN_P, c, y, dev_yp), pair_copy(S_OWN_M, c, y, dev_ym)]
+        return [pair_copy(S_PAIR_P, c, y, dev_yp), pair_copy(S_PAIR_M, c, y, dev_ym)]
 
     def pair_recv(c):
-        return [pair_copy(S_OWN_P, c, ym, dev_yp), pair_copy(S_OWN_M, c, yp, dev_ym)]
+        return [pair_copy(S_PAIR_P, c, ym, dev_yp), pair_copy(S_PAIR_M, c, yp, dev_ym)]
 
     def fwd_send(c):
         return [half_copy(S_FWD_P, c, ym, 0, dev_yp), half_copy(S_FWD_M, c, yp, 1, dev_ym)]
@@ -176,7 +175,7 @@
 
     def out_copy(c):
         return pltpu.make_async_copy(
-            out.at[c], coef.at[pl.ds(pl.multiple_of(c * 8, 8), 8)], osem.at[c])
+            out.at[pl.ds(pl.multiple_of(c * 8, 8), 8)], coef.at[pl.ds(pl.multiple_of(c * 8, 8), 8)], osem.at[0])
 
     def start(copies):
         for copy in copies:
@@ -200,15 +199,6 @@
         return pltpu.make_async_remote_copy(
             src_ref=shs.at[h], dst_ref=sb.at[n], send_sem=shs_s.at[h], recv_sem=shs_r.at[n],
             device_id=(s, 2 * s + h), device_id_type=MESH)
-
-    for h in range(2):
-        @pl.when(n != 2 * s + h)
-        def _(h=h):
-            shs_copy(h).start()
-
-        @pl.when(n == 2 * s + h)
-        def _(h=h):
-            sb[n] = shs[h]
 
     def split_piece(i):
         def body(r, carry):
@@ -248,19 +238,6 @@
     for j in range(NNEUR):
         piece = row_piece(bias_row, j * spec_rows, spec_rows)
         bias16[j:j + 1, :] = jnp.where(lane < spec_rows, piece, 0.0)
-    columns = (n * kdim).astype(F32)
-    for b in range(2):
-        for q in range(4):
-            row = row_piece(names[b:b + 1, :].astype(F32), q * spec_rows, spec_rows)
-            row = jnp.broadcast_to(jnp.where(lane < spec_rows, row, -1.0), (LANES, LANES))
-            target = row.T - columns
-            for t in range(kdim // LANES):
-                ids = lax.broadcasted_iota(jnp.int32, (LANES, LANES), 1).astype(F32) + float(t * LANES)
-                hit = jnp.where(target == ids, 1.0, 0.0)
-                onehot[b, q * LANES:(q + 1) * LANES, t * LANES:(t + 1) * LANES] = hit.astype(BF16)
-        total = jnp.dot(jnp.ones((16, 4 * LANES), BF16), onehot[b], preferred_element_type=F32)
-        touched[b:b + 1, :] = total[0:1, :]
-
     def shift_recv():
         for j in range(1, NNEUR):
             other = (n + j) % NNEUR
@@ -272,11 +249,12 @@
     row8 = lax.broadcasted_iota(jnp.int32, (8, LANES), 0)
     lane8 = lax.broadcasted_iota(jnp.int32, (8, LANES), 1)
 
-    def multiply(c):
-        a = g[c].reshape(16 * NSPEC, kdim)
-        hi = a.astype(BF16)
-        asp[0:16 * NSPEC, :] = hi
-        asp[16 * NSPEC:, :] = (a - hi.astype(F32)).astype(BF16)
+    def multiply(c, part):
+        if part == 0:
+            a = g[c].reshape(16 * NSPEC, kdim)
+            hi = a.astype(BF16)
+            asp[0:16 * NSPEC, :] = hi
+            asp[16 * NSPEC:, :] = (a - hi.astype(F32)).astype(BF16)
 
         def tile(j, carry):
             cols = pl.ds(pl.multiple_of(j * TILE_N, TILE_N), TILE_N)
@@ -286,29 +264,25 @@
             prod[c, :, :, :, :, cols] = res.reshape(XL, Z, 2, 8, TILE_N)
             return carry
 
-        lax.fori_loop(0, ndim // TILE_N, tile, 0)
+        half_tiles = ndim // TILE_N // 2
+        lax.fori_loop(part * half_tiles, (part + 1) * half_tiles, tile, 0)
 
     def stage(cond, body):
         pl.when(cond)(body)
 
-    def drain(c):
-        xh_send(c).wait_send()
-        core_copy(c).wait_send()
-        xl_copy(c).wait_send()
-        out_copy(c).wait()
-        for copies in (fwd_send(c), z1_copy(c), z2_copy(c)):
-            for copy in copies:
-                copy.wait_send()
-
-        @pl.when(c < LOOK_PAR)
-        def _():
-            for copy in own_send(c) + par_send(c):
-                copy.wait_send()
-
-        @pl.when(c >= LOOK_PAR)
-        def _():
-            for copy in pair_send(c):
-                copy.wait_send()
+    def find_columns():
+        columns = (n * kdim).astype(F32)
+        for b in range(2):
+            for q in range(4):
+                row = row_piece(names[b:b + 1, :].astype(F32), q * spec_rows, spec_rows)
+                row = jnp.broadcast_to(jnp.where(lane < spec_rows, row, -1.0), (LANES, LANES))
+                target = row.T - columns
+                for t in range(kdim // LANES):
+                    ids = lax.broadcasted_iota(jnp.int32, (LANES, LANES), 1).astype(F32) + float(t * LANES)
+                    hit = jnp.where(target == ids, 1.0, 0.0)
+                    onehot[b, q * LANES:(q + 1) * LANES, t * LANES:(t + 1) * LANES] = hit.astype(BF16)
+            total = jnp.dot(jnp.ones((16, 4 * LANES), BF16), onehot[b], preferred_element_type=F32)
+            touched[b:b + 1, :] = total[0:1, :]
 
     def iteration(t, carry):
         @pl.when(t + LOOK_PAR < chunks)
@@ -337,8 +311,7 @@
         @pl.when(t < chunks)
         def _():
             wait_recv(fwd_recv(t))
-            multiply(t)
-            core_copy(t).start()
+            multiply(t, 0)
 
         @pl.when(jnp.logical_and(t >= 1, t - 1 < chunks))
         def _():
@@ -347,6 +320,11 @@
             for a in range(XL):
                 prod[c, a, z2, k] = prod[c, a, z2, k] + cr[c, a, z2]
             start(z1_copy(c))
+
+        @pl.when(t < chunks)
+        def _():
+            multiply(t, 1)
+            core_copy(t).start()
 
         @pl.when(jnp.logical_and(t >= LAG_Z2, t - LAG_Z2 < chunks))
         def _():
@@ -361,6 +339,10 @@
                     prod[c, a, zm, k, :, half:] + cr[c, a, zm, :, half:] + z1m[c, a])
             start(z2_copy(c))
 
+        @pl.when(t == chunks + LAG_Z2 - 1)
+        def _():
+            find_columns()
+
         @pl.when(jnp.logical_and(t >= LAG_FIN, t - LAG_FIN < chunks))
         def _():
             c = t - LAG_FIN
@@ -369,21 +351,28 @@
                 prod[c, a, z, k] = prod[c, a, z, k] + cr[c, a, z] + z2p[c, a] + z2m[c, a]
             xl_copy(c).start()
 
-        @pl.when(t > LAG_OUT)
-        def _():
-            drain(t - LAG_OUT - 1)
-
         @pl.when(t >= LAG_OUT)
         def _():
             c = t - LAG_OUT
             xl_copy(c).wait_recv()
             v = prod[c, xl, z, k] + xb[c]
-            out[c] = v
+            out[pl.ds(pl.multiple_of(c * 8, 8), 8), :] = v
             out_copy(c).start()
             total = jnp.sum(fold_lanes(v * in_center - jnp.abs(v) * in_radius), axis=1, keepdims=True)
             tb[...] += jnp.where(lane8 == row8 + c * 8, jnp.broadcast_to(total, (8, LANES)), 0.0)
 
-        @pl.when(jnp.logical_and(t == 2, n // 2 == s))
+        @pl.when(t == LAG_OUT + 1)
+        def _():
+            for h in range(2):
+                @pl.when(n != 2 * s + h)
+                def _(h=h):
+                    shs_copy(h).start()
+
+                @pl.when(n == 2 * s + h)
+                def _(h=h):
+                    sb[n] = shs[h]
+
+        @pl.when(jnp.logical_and(t == LAG_OUT + 4, n // 2 == s))
         def _():
             shift_recv()
             total = sb[0]
@@ -421,7 +410,26 @@
     for j in range(1, NNEUR):
         bb_copy(j, n).start()
 
-    drain(chunks - 1)
+    def sent(src, kind):
+        pltpu.make_async_remote_copy(
+            src_ref=src, dst_ref=src, send_sem=ssem.at[kind], recv_sem=rsem.at[0, kind],
+            device_id=dev_core, device_id_type=MESH).wait_send()
+
+    rest = pl.ds(LOOK_PAR, chunks - LOOK_PAR)
+    sent(g.at[:, xh, y], S_XH)
+    for kind in (S_OWN_P, S_OWN_M, S_PAR_P, S_PAR_M):
+        sent(g.at[pl.ds(0, LOOK_PAR), xh, y], kind)
+    for kind in (S_PAIR_P, S_PAIR_M):
+        sent(g.at[rest, :, y], kind)
+    for kind in (S_FWD_P, S_FWD_M):
+        sent(g.at[:, :, y, 0], kind)
+    sent(prod.at[:, :, :, 1 - k], S_CORE)
+    for kind in (S_Z1_P, S_Z1_M):
+        sent(prod.at[:, :, z2, k, :, pl.ds(0, half)], kind)
+    for kind in (S_Z2_P, S_Z2_M):
+        sent(prod.at[:, :, z, k], kind)
+    sent(prod.at[:, 1 - xl, z, k], S_XL)
+    pltpu.make_async_copy(out, coef, osem.at[0]).wait()
     for h in range(2):
         @pl.when(n != 2 * s + h)
         def _(h=h):
@@ -507,9 +515,9 @@
             pltpu.VMEM((2, 4 * LANES, kdim), BF16),
             pltpu.VMEM((2, kdim), F32),
             pltpu.VMEM((NNEUR, LANES), F32),
-            pltpu.VMEM((chunks, 8, ndim), F32),
-            dma((11 + kdim // W_ROWS,)), dma((chunks,)),
-            dma((chunks, NCOPY)), dma((chunks, NCOPY)),
+            pltpu.VMEM((hrows, ndim), F32),
+            dma((11 + kdim // W_ROWS,)), dma((1,)),
+            dma((NCOPY,)), dma((chunks, NCOPY)),
             dma((2,)), dma((NNEUR,)),
             dma((NSPEC,)), dma((NSPEC,)),
             dma((NNEUR,)), dma((NNEUR,)),

time: 104 us -> 98.6 us (0.948)
  Pallas kernels: 103 us -> 97.8 us
    pallas_call x1, Pallas kernels: 101 us -> 95.8 us  [per_device(): pl.pallas_call(kernel, out_shape=(jax.ShapeDtypeStruct((hrows, ndim), F32...]
where the time goes in v3:
time: 98.6 us; the launch traced here: 98.5 us
  Pallas kernels  97.8 us (99%)
    pallas_call x1, Pallas kernels, per_device(): pl.pallas_call(kernel, out_shape=(jax.ShapeDtypeStruct((hrows, ndim), F32...  95.8 us
    pallas_call x1, Pallas kernels, hand_on(): pl.pallas_call(copy_kernel, out_shape=tuple((jax.ShapeDtypeStruct(a.shape...  2.04 us

profile of v3, /device:TPU:1, one launch (start us, length us, event | category | flops | bytes accessed | tf_op | source)
XLA Modules:
  0.0 98.5 jit_solution(8006866522736584469)
XLA Ops:
  0.6 95.8 %shard_map.147 = (f32[96,2048]{1,0:T(8,128)}, f32[1,96]{1,0:T(1,128)}, f32[2,1024]{1,0:T(2,128)}, f32[2,1024]{1,0:T(2,128)}) custom-call(f32[2,96,1024]{2,1,0:T(8,128)} %bitcast.4, f32[1024,2048]{1,0:T(8,128)} %weight.1, f32[1,1024]{1,0:T(1,128)} %bitcast.6, f32[2,1024]{1,0:T(2,128)} %rest_1_.1, f32[2,1024]{1,0:T(2,128)} %rest_2_.1, f32[2,1024]{1,0:T(2,128)} %rest_3_.1, ...), custom_call_target="tpu_custom_call" | custom-call | flops 19327352832 | bytes 8388608 | tf_op jit(solution)/shard_map/pallas_call | solution.py:485
  96.4 2.0 %shard_map.148 = (f32[96,2048]{1,0:T(8,128)}, f32[1,96]{1,0:T(1,128)}, f32[2,1024]{1,0:T(2,128)}, f32[2,1024]{1,0:T(2,128)}) custom-call(f32[96,2048]{1,0:T(8,128)} %get-tuple-element.12.refs_0_, f32[1,96]{1,0:T(1,128)} %get-tuple-element.13.refs_1_, f32[2,1024]{1,0:T(2,128)} %get-tuple-element.14.refs_2_, f32[2,1024]{1,0:T(2,128)} %get-tuple-element.15.refs_3_), custom_call_target="tpu_custom_call" | custom-call | tf_op jit(solution)/shard_map/pallas_call | solution.py:559

commit v4 on v3

--- a/solution.py
+++ b/solution.py
@@ -257,15 +257,14 @@
             asp[16 * NSPEC:, :] = (a - hi.astype(F32)).astype(BF16)
 
         def tile(j, carry):
-            cols = pl.ds(pl.multiple_of(j * TILE_N, TILE_N), TILE_N)
+            cols = pl.ds(j * TILE_N, TILE_N)
             both = jnp.dot(asp[...], whi[:, cols], preferred_element_type=F32)
             rest = jnp.dot(asp[0:16 * NSPEC, :], wlo[:, cols], preferred_element_type=F32)
             res = both[0:16 * NSPEC] + both[16 * NSPEC:] + rest
             prod[c, :, :, :, :, cols] = res.reshape(XL, Z, 2, 8, TILE_N)
             return carry
 
-        half_tiles = ndim // TILE_N // 2
-        lax.fori_loop(part * half_tiles, (part + 1) * half_tiles, tile, 0)
+        tile(part, 0)
 
     def stage(cond, body):
         pl.when(cond)(body)
@@ -386,15 +385,19 @@
 
     pb[s] = tb[...]
 
-    def pb_copy(j, src):
+    def spec_at(dx, dy):
+        return (xh + dx) % XH * Y + (y + dy) % Y
+
+    def pb_copy(dx, dy, src):
         return pltpu.make_async_remote_copy(
-            src_ref=pb.at[src], dst_ref=pb.at[src], send_sem=pb_s.at[j], recv_sem=pb_r.at[j],
-            device_id=((s + j) % NSPEC, n), device_id_type=MESH)
-
-    for j in range(1, NSPEC):
-        pb_copy(j, s).start()
-    for j in range(1, NSPEC):
-        pb_copy(j, (s + NSPEC - j) % NSPEC).wait_recv()
+            src_ref=pb.at[src], dst_ref=pb.at[src], send_sem=pb_s.at[dx * Y + dy],
+            recv_sem=pb_r.at[dx * Y + dy], device_id=(spec_at(dx, dy), n), device_id_type=MESH)
+
+    spec_steps = [(1, 2), (1, 1), (1, 3), (1, 0), (0, 2), (0, 1), (0, 3)]
+    for dx, dy in spec_steps:
+        pb_copy(dx, dy, s).start()
+    for dx, dy in spec_steps:
+        pb_copy(dx, dy, spec_at(-dx + XH, -dy + Y)).wait_recv()
     bound = pb[0]
     for j in range(1, NSPEC):
         bound = bound + pb[j]
@@ -402,13 +405,19 @@
     bb[n] = bound
     lbound[...] = bound[0:1, 0:lbound.shape[1]]
 
-    def bb_copy(j, src):
+    def neuron_at(dx, dz, dk):
+        return (xl + dx) % XL * 2 * Z + (z + dz) % Z * 2 + (k + dk) % 2
+
+    def bb_copy(dx, dz, dk, src):
+        at = dx * 2 * Z + dz * 2 + dk
         return pltpu.make_async_remote_copy(
-            src_ref=bb.at[src], dst_ref=bb.at[src], send_sem=bb_s.at[j], recv_sem=bb_r.at[j],
-            device_id=(s, (n + j) % NNEUR), device_id_type=MESH)
-
-    for j in range(1, NNEUR):
-        bb_copy(j, n).start()
+            src_ref=bb.at[src], dst_ref=bb.at[src], send_sem=bb_s.at[at], recv_sem=bb_r.at[at],
+            device_id=(s, neuron_at(dx, dz, dk)), device_id_type=MESH)
+
+    neuron_steps = [(dx, dz, dk) for dx, dz in ((1, 2), (1, 1), (1, 3), (0, 2), (1, 0), (0, 1), (0, 3), (0, 0))
+                    for dk in (1, 0) if (dx, dz, dk) != (0, 0, 0)]
+    for step in neuron_steps:
+        bb_copy(*step, n).start()
 
     def sent(src, kind):
         pltpu.make_async_remote_copy(
@@ -435,8 +444,8 @@
         def _(h=h):
             shs_copy(h).wait_send()
 
-    for j in range(1, NNEUR):
-        bb_copy(j, (n + NNEUR - j) % NNEUR).wait_recv()
+    for dx, dz, dk in neuron_steps:
+        bb_copy(dx, dz, dk, neuron_at(-dx + XL, -dz + Z, -dk + 2)).wait_recv()
 
     row = lax.broadcasted_iota(jnp.int32, (8, 4 * LANES), 0)
 
@@ -463,10 +472,10 @@
         nslope[b:b + 1, :] = slope
         nshift[b:b + 1, :] = slope * falling
 
-    for j in range(1, NSPEC):
-        pb_copy(j, s).wait_send()
-    for j in range(1, NNEUR):
-        bb_copy(j, n).wait_send()
+    for dx, dy in spec_steps:
+        pb_copy(dx, dy, s).wait_send()
+    for step in neuron_steps:
+        bb_copy(*step, n).wait_send()
 
 
 def per_device(panel, weight, layer_bias, act_center, act_radius, alpha, in_center, in_radius,

time: 98.6 us -> 98.5 us (level)
  no operation moved by 1% of the time
where the time goes in v4:
time: 98.5 us; the launch traced here: 98.4 us
  Pallas kernels  97.8 us (99%)
    pallas_call x1, Pallas kernels, per_device(): pl.pallas_call(kernel, out_shape=(jax.ShapeDtypeStruct((hrows, ndim), F32...  95.7 us
    pallas_call x1, Pallas kernels, hand_on(): pl.pallas_call(copy_kernel, out_shape=tuple((jax.ShapeDtypeStruct(a.shape...  2.04 us

profile of v4, /device:TPU:1, one launch (start us, length us, event | category | flops | bytes accessed | tf_op | source)
XLA Modules:
  0.0 98.4 jit_solution(2256598806463044856)
XLA Ops:
  0.6 95.7 %shard_map.147 = (f32[96,2048]{1,0:T(8,128)}, f32[1,96]{1,0:T(1,128)}, f32[2,1024]{1,0:T(2,128)}, f32[2,1024]{1,0:T(2,128)}) custom-call(f32[2,96,1024]{2,1,0:T(8,128)} %bitcast.4, f32[1024,2048]{1,0:T(8,128)} %weight.1, f32[1,1024]{1,0:T(1,128)} %bitcast.6, f32[2,1024]{1,0:T(2,128)} %rest_1_.1, f32[2,1024]{1,0:T(2,128)} %rest_2_.1, f32[2,1024]{1,0:T(2,128)} %rest_3_.1, ...), custom_call_target="tpu_custom_call" | custom-call | flops 19327352832 | bytes 8388608 | tf_op jit(solution)/shard_map/pallas_call | solution.py:494
  96.4 2.0 %shard_map.148 = (f32[96,2048]{1,0:T(8,128)}, f32[1,96]{1,0:T(1,128)}, f32[2,1024]{1,0:T(2,128)}, f32[2,1024]{1,0:T(2,128)}) custom-call(f32[96,2048]{1,0:T(8,128)} %get-tuple-element.12.refs_0_, f32[1,96]{1,0:T(1,128)} %get-tuple-element.13.refs_1_, f32[2,1024]{1,0:T(2,128)} %get-tuple-element.14.refs_2_, f32[2,1024]{1,0:T(2,128)} %get-tuple-element.15.refs_3_), custom_call_target="tpu_custom_call" | custom-call | tf_op jit(solution)/shard_map/pallas_call | solution.py:568
